TPU v7x, 256 devices: a whole 4x4x8 slice. The times are simulated.
256 devices in a mesh: patch: 8 (over y, core), visit: 32 (over x, z).
Axes of the slice: x: 4, y: 4, z: 8, core: 2. Of those that a mesh axis runs over, the one named last changes fastest.
Arguments:
- images: bfloat16 [8192, 128, 128], P(('patch', 'visit')), may hold values from -6 to 6
- variances: bfloat16 [8192, 128, 128], P(('patch', 'visit')), may hold values from 0.5 to 4
- bad_pixels: int32 [8192, 128, 128], P(('patch', 'visit')), may hold values 0 or 1
- routes: int32 [8192, 1], P(('patch', 'visit')), may hold values from 0 to 7; in each aligned block of 32 rows (0 to 31, 32 to 63, ...) at most 8 rows name the same one
- offsets: int32 [8192, 2], P(('patch', 'visit')), may hold values from 0 to 112
- tile_visits: int32 [8192], P(('patch', 'visit')), may hold values from 0 to 1
- coefficients: bfloat16 [64, 3, 16], P('visit'), may hold values from -1.5 to 1.5
- kernel_counts: int32 [64], P('visit'), may hold values from 1 to 16
- taps: bfloat16 [16, 2, 41], replicated, may hold values from -0.796875 to 0.796875
Outputs:
- coadd: float32 [8192, 1024], P(('patch', 'visit'))
- depth: float32 [8192, 1024], P(('patch', 'visit'))
Inputs may be any that keep to these rules, and one draw needn't show every extreme that they name: `routes`: in the rows of one device at most 8 tiles intersect one patch, and exactly 8 intersect one patch on some device.
All inputs are finite; a program needn't handle non-finite values. No bound on the sum of `bad_pixels` on one device may be relied on, other than what follows from the above.
Results may differ from a plain program's by a relative error of at most 0.0046.
Values may be sent and summed in bfloat16 or wider, within the bound.
A program may use at most 64 MiB of HBM per device.

v0:
```python
import jax
import jax.numpy as jnp
from jax import lax
from jax.sharding import PartitionSpec as P

WIN = 1024


HIGHEST = lax.Precision.HIGHEST


def band_matrices(taps, tile_side):
    tap_span = taps.shape[2]
    grid = (tap_span, tile_side, tile_side)
    tap_index = lax.broadcasted_iota(jnp.int32, grid, 0)
    row_iota = lax.broadcasted_iota(jnp.int32, grid, 1)
    col_iota = lax.broadcasted_iota(jnp.int32, grid, 2)
    lookup = (col_iota - row_iota + tap_span // 2 == tap_index).astype(jnp.float32)
    taps_wide = taps.astype(jnp.float32)
    vertical = jnp.einsum("kt,tij->kij", taps_wide[:, 0, :], lookup, precision=HIGHEST).astype(
        jnp.bfloat16
    )
    horizontal = jnp.einsum("kt,tij->kij", taps_wide[:, 1, :], lookup, precision=HIGHEST).astype(
        jnp.bfloat16
    )
    return (vertical, horizontal)


def match_tiles(images, tile_coefs, anchors, vertical, horizontal):
    tile_side = images.shape[1]
    pixel_iota = lax.iota(jnp.float32, tile_side)

    def match_single(item):
        image, coefs, anchor = item
        blurred = jnp.einsum(
            "kij,jw->kiw", vertical, image, preferred_element_type=jnp.float32
        ).astype(jnp.bfloat16)
        smoothed = jnp.einsum(
            "kiw,kvw->kiv", blurred, horizontal, preferred_element_type=jnp.float32
        )
        terms = jnp.einsum("ck,kiv->civ", coefs, smoothed, precision=HIGHEST)
        row_place = (anchor[0] + pixel_iota) / WIN
        col_place = (anchor[1] + pixel_iota) / WIN
        matched = terms[0] + row_place[:, None] * terms[1] + col_place[None, :] * terms[2]
        return matched.astype(jnp.bfloat16)

    return lax.map(match_single, (images, tile_coefs, anchors), batch_size=4)


def local(
    images, variances, bad_pixels, routes, offsets, tile_visits, coefficients, kernel_counts, taps
):
    patches = lax.axis_size("patch")
    tile_count = images.shape[0]
    tile_side = images.shape[1]
    capacity = 2 * tile_count // patches
    nbasis = taps.shape[0]
    vertical, horizontal = band_matrices(taps, tile_side)
    weights = jnp.where(bad_pixels == 0, 1.0 / variances.astype(jnp.float32), 0.0).astype(
        jnp.bfloat16
    )
    visit_pick = (
        tile_visits[:, None] == lax.iota(jnp.int32, coefficients.shape[0])[None, :]
    ).astype(jnp.float32)
    active = (lax.iota(jnp.int32, nbasis)[None, :] < kernel_counts[:, None]).astype(jnp.float32)
    visit_coefs = coefficients.astype(jnp.float32) * active[:, None, :]
    tile_coefs = jnp.einsum("tv,vck->tck", visit_pick, visit_coefs, precision=HIGHEST)
    targets = routes[:, 0]
    onehot = (targets[:, None] == lax.iota(jnp.int32, patches)[None, :]).astype(jnp.int32)
    earlier = jnp.sum((jnp.cumsum(onehot, axis=0) - onehot) * onehot, axis=1)
    slot_index = targets * capacity + earlier
    selector = (lax.iota(jnp.int32, patches * capacity)[:, None] == slot_index[None, :]).astype(
        jnp.bfloat16
    )

    def to_slots(values):
        flat = values.reshape(tile_count, -1)
        placed = jnp.dot(selector, flat, preferred_element_type=jnp.float32).astype(jnp.bfloat16)
        return placed.reshape((patches, capacity) + values.shape[1:])

    meta = jnp.concatenate(
        [tile_coefs.reshape(tile_count, -1), offsets.astype(jnp.float32)], axis=1
    ).astype(jnp.bfloat16)
    got_images = lax.all_to_all(to_slots(images), "patch", split_axis=0, concat_axis=0, tiled=True)
    got_weights = lax.all_to_all(
        to_slots(weights), "patch", split_axis=0, concat_axis=0, tiled=True
    )
    got_meta = lax.all_to_all(to_slots(meta), "patch", split_axis=0, concat_axis=0, tiled=True)
    leading = got_images.shape[:2]
    flat_meta = got_meta.reshape(-1, got_meta.shape[2]).astype(jnp.float32)
    coefs = flat_meta[:, : 3 * nbasis].reshape(-1, 3, nbasis)
    corners = 8.0 * flat_meta[:, 3 * nbasis :]
    matched_flat = match_tiles(
        got_images.reshape(-1, tile_side, tile_side), coefs, corners, vertical, horizontal
    )
    matched, got_weights, corners = (
        matched_flat.reshape(leading + (tile_side, tile_side)),
        got_weights,
        corners.reshape(leading + (2,)),
    )
    slot_values = matched.reshape(-1, tile_side, tile_side)
    slot_weights = got_weights.reshape(-1, tile_side, tile_side)
    slot_corners = corners.reshape(-1, 2).astype(jnp.int32)

    def add_slot(position, inner):
        numer, denom = inner
        top = slot_corners[position, 0]
        left = slot_corners[position, 1]
        weight_tile = slot_weights[position].astype(jnp.float32)
        value_tile = slot_values[position].astype(jnp.float32)
        numer = lax.dynamic_update_slice(
            numer,
            lax.dynamic_slice(numer, (top, left), (tile_side, tile_side))
            + weight_tile * value_tile,
            (top, left),
        )
        denom = lax.dynamic_update_slice(
            denom,
            lax.dynamic_slice(denom, (top, left), (tile_side, tile_side)) + weight_tile,
            (top, left),
        )
        return (numer, denom)

    empty = jnp.zeros((WIN, WIN), jnp.float32)
    local_numer, local_denom = lax.fori_loop(0, slot_values.shape[0], add_slot, (empty, empty))
    numer, denom = (
        lax.psum_scatter(local_numer, "visit", scatter_dimension=0, tiled=True),
        lax.psum_scatter(local_denom, "visit", scatter_dimension=0, tiled=True),
    )
    coadd = numer / jnp.maximum(denom, 1.0)
    return (coadd, denom)


def solution(mesh):
    return jax.shard_map(
        local,
        mesh=mesh,
        in_specs=(
            P(("patch", "visit"), None, None),
            P(("patch", "visit"), None, None),
            P(("patch", "visit"), None, None),
            P(("patch", "visit"), None),
            P(("patch", "visit"), None),
            P(("patch", "visit")),
            P("visit", None, None),
            P("visit"),
            P(),
        ),
        out_specs=(P(("patch", "visit"), None), P(("patch", "visit"), None)),
        check_vma=False,
    )
```

profile of v0, /device:TPU:24, one launch (start us, length us, event | category | flops | bytes accessed | tf_op | source)
XLA Modules:
  0.0 1446.2 jit_solution(8840598971635958585)
XLA Ops:
  12.7 5.2 all-to-all-start
  21.3 5.5 all-to-all-start.2
  32.5 19.4 %all-to-all-done.2 = bf16[8,8,128,128]{3,1,2,0:T(8,128)(2,1)S(1)} async-done(((bf16[8,8,128,128]{3,1,2,0:T(8,128)(2,1)}), bf16[8,8,128,128]{3,1,2,0:T(8,128)(2,1)S(1)}, u32[]{:S(2)}, u32[]{:S(2)}) %all-to-all-start.2) | async-done | bytes 2097184 | tf_op jit(solution)/shard_map/all_to_all | solution.py:84
  53.2 5.6 all-to-all-start.1
  62.3 158.4 %while.28 = (s32[]{:T(128)}, bf16[16,4,128,128]{3,2,1,0:T(8,128)(2,1)}, f32[16,4,3,16]{3,2,1,0:T(4,128)S(1)}, bf16[16,4,128,128]{3,2,1,0:T(8,128)(2,1)}, bf16[16...) while((s32[]{:T(128)}, ...), condition=%wide.region_3.4_spmd.clone.clone, body=%wide.region_2.3_spmd.clone.clone.sunk | while | flops 574949376 | bytes 21250316 | solution.py:47
  66.5 4.4 fusion.76
  76.4 4.4 fusion.76
  86.3 4.4 fusion.76
  96.2 4.4 fusion.76
  106.1 4.4 fusion.76
  116.0 4.4 fusion.76
  125.9 4.4 fusion.76
  135.8 4.4 fusion.76
  145.7 4.4 fusion.76
  155.6 4.4 fusion.76
  165.4 4.4 fusion.76
  175.3 4.4 fusion.76
  185.3 4.4 fusion.76
  195.2 4.4 fusion.76
  205.1 4.4 fusion.76
  215.0 4.4 fusion.76
  227.7 746.0 %while.27 = (s32[]{:T(128)}, f32[1024,1024]{1,0:T(8,128)}, f32[1024,1024]{1,0:T(8,128)}, s32[64,2]{0,1:T(2,128)S(1)}, bf16[64,128,128]{2,1,0:T(8,128)(2,1)}, /*i...) while((s32[]{:T(128)}, f32[1024,1024]{1,0:T(8,128)}, f32[1024,1024]{1,0:T(8,128)}, ...), condition=%wide.region_5.6_spmd, body=%wide.region_4.5_spmd.sunk | while | flops 81928 | bytes 590033 | solution.py:125
  974.5 239.5 %reduce-scatter.5.cloned.1.call-done = f32[32,1024]{1,0:T(8,128)} async-done(((f32[1024,1024]{1,0:T(8,128)}), f32[32,1024]{1,0:T(8,128)}) %reduce-scatter.5.cloned.1.call-update) | async-done | bytes 131088 | tf_op jit(solution)/shard_map/reduce_scatter | solution.py:128
  1214.0 223.8 %reduce-scatter.3.cloned.1.call-done = f32[32,1024]{1,0:T(8,128)} async-done(((f32[1024,1024]{1,0:T(8,128)}), f32[32,1024]{1,0:T(8,128)}) %reduce-scatter.3.cloned.1.call-update) | async-done | bytes 131088 | tf_op jit(solution)/shard_map/reduce_scatter | solution.py:127
  (428 shorter events, 619.6 us)
Async XLA Ops:
  12.7 8.6 all-to-all-start
  21.3 5.5 copy-start.3
  21.3 30.6 %all-to-all-start.2 = ((bf16[8,8,128,128]{3,1,2,0:T(8,128)(2,1)}), bf16[8,8,128,128]{3,1,2,0:T(8,128)(2,1)S(1)}, u32[]{:S(2)}, u32[]{:S(2)}) async-start(bf16[8,8,128,128]{3,1,2,0:T(8,128)(2,1)} %fusion.24), calls=%async_computation.2 | async-start | bytes 4194304 | tf_op jit(solution)/shard_map/all_to_all | solution.py:84
  27.5 1.6 copy-start.1
  27.5 1.8 copy-start.2
  51.9 1.3 copy-start
  53.2 167.5 %all-to-all-start.1 = ((bf16[8,8,128,128]{3,1,2,0:T(8,128)(2,1)}), bf16[8,8,128,128]{3,1,2,0:T(8,128)(2,1)S(1)}, u32[]{:S(2)}, u32[]{:S(2)}) async-start(bf16[8,8,128,128]{3,1,2,0:T(8,128)(2,1)} %fusion.23), calls=%async_computation.1 | async-start | bytes 4194304 | tf_op jit(solution)/shard_map/all_to_all | solution.py:85
  58.9 1155.1 %reduce-scatter.5.cloned.1.call-start = ((), (), s32[]{:S(2)}) async-start(), calls=%async_computation.6 | async-start | bytes 4325376 | tf_op jit(solution)/shard_map/reduce_scatter | solution.py:128
  973.7 464.0 %reduce-scatter.3.cloned.1.call-start = ((), (), s32[]{:S(2)}) async-start(), calls=%async_computation.5 | async-start | bytes 4325376 | tf_op jit(solution)/shard_map/reduce_scatter | solution.py:127
Sparse Core Ops, SparseCore 0:
  973.9 240.0 reduce-scatter.4
  1218.4 219.3 reduce-scatter.2
where the time goes:
time: 1470 us; the launch traced here: 1450 us
  waiting for transfers between devices  483 us (33%)
  local copies, waits for them, and re-layouts  476 us (32%)
  loops' own time  244 us (17%)
  matrix products  120 us (8%)
  other arithmetic  92 us (6%)
  starting transfers between devices  16.4 us (1%)
    another operation x1, loops' own time, local(): lax.fori_loop(0, slot_values.shape[0], add_slot, (empty, empty))  243 us
    reduce_scatter x1, waiting for transfers between devices, local(): lax.psum_scatter(local_denom, 'visit', scatter_dimension=0, tiled=True)  239 us
    reduce_scatter x1, waiting for transfers between devices, local(): lax.psum_scatter(local_numer, 'visit', scatter_dimension=0, tiled=True)  224 us
    dynamic_update_slice x64, local copies, waits for them, and re-layouts, add_slot(): lax.dynamic_update_slice(numer, lax.dynamic_slice(numer, (top, left), (ti...  198 us
    dynamic_update_slice x64, local copies, waits for them, and re-layouts, add_slot(): lax.dynamic_update_slice(denom, lax.dynamic_slice(denom, (top, left), (ti...  195 us
    add x64, other arithmetic, add_slot(): lax.dynamic_slice(denom, (top, left), (tile_side, tile_side)) + weight_tile  72.4 us
    dot_general x16, matrix products, match_single(): terms = jnp.einsum('ck,kiv->civ', coefs, smoothed, precision=HIGHEST)  69.8 us
    dynamic_slice x64, local copies, waits for them, and re-layouts, add_slot(): left = slot_corners[position, 1]  37.9 us
  transfers between devices with their start and end apart: 5, of which 3 were waited for; matrix products, arithmetic and copies ran while one was open for 12% of the time, Pallas kernels for 0%

commit v1 on v0

v1 whole, which is shorter than its diff:
```python
import functools

import jax
import jax.numpy as jnp
from jax import lax
from jax.experimental import pallas as pl
from jax.experimental.pallas import tpu as pltpu
from jax.sharding import PartitionSpec as P

TS = 128
WIN = 1024
CAP = 8
NB = 16
NT = 32
NP = 8
NX = 4
NZ = 8
ROWS = 32
HALF = WIN // 2
MESH = pl.DeviceIdType.MESH
BF16 = jnp.bfloat16
F32 = jnp.float32
VMEM = pl.BlockSpec(memory_space=pltpu.VMEM)
SMEM = pl.BlockSpec(memory_space=pltpu.SMEM)
ANY = pl.BlockSpec(memory_space=pl.ANY)


def band(row):
    wide = jnp.broadcast_to(row, (TS, 2 * TS))
    return pltpu.roll(wide, 0, 1, stride=1, stride_axis=0)[:, :TS].astype(BF16)


def greet(axis, others):
    barrier = pltpu.get_barrier_semaphore()
    for other in others:
        pl.semaphore_signal(barrier, inc=1, device_id={axis: other}, device_id_type=MESH)


def front_kernel(
    table, coefs, rolls, meta, img_in, var_in, bad_in, wgt_out, mat_out, meta_out,
    img, var, bad, wslots, tiles, vert, horz, lm, in_sem, own_sem, send_sem, recv_sem,
):
    me = lax.axis_index("patch")
    loads = [
        pltpu.make_async_copy(src, dst, in_sem.at[i])
        for i, (src, dst) in enumerate(((var_in, var), (bad_in, bad), (img_in, img)))
    ]
    for load in loads:
        load.start()
    greet("patch", [lax.rem(me + d, NP) for d in range(1, NP)])
    pl.semaphore_wait(pltpu.get_barrier_semaphore(), NP - 1)
    loads[0].wait()
    loads[1].wait()

    def weigh(j, carry):
        t = table[j]
        weight = jnp.where(bad[t] == 0, 1.0 / var[t].astype(F32), 0.0)
        wslots[j] = weight.astype(BF16)
        return carry

    copies = []
    for d in (4, 3, 5, 2, 6, 1, 7, 0):
        there = lax.rem(me + d, NP)
        lax.fori_loop(there * CAP, there * CAP + CAP, weigh, 0)
        block = wslots.at[pl.ds(there * CAP, CAP)]
        if d == 0:
            own = [
                pltpu.make_async_copy(block, wgt_out.at[me], own_sem.at[0]),
                pltpu.make_async_copy(meta.at[me], meta_out.at[me], own_sem.at[1]),
            ]
            for c in own:
                c.start()
            continue
        for i, (src, dst) in enumerate(((meta.at[there], meta_out), (block, wgt_out))):
            copies.append(
                pltpu.make_async_remote_copy(
                    src_ref=src,
                    dst_ref=dst.at[me],
                    send_sem=send_sem.at[i, d],
                    recv_sem=recv_sem.at[i, d],
                    device_id={"patch": there},
                    device_id_type=MESH,
                )
            )
            copies[-1].start()

    horz[...] = jnp.zeros_like(horz)
    for k in range(NB):
        vert[k * TS : (k + 1) * TS, :] = band(rolls[k : k + 1, :])
        half = slice((k % 2) * TS, (k % 2 + 1) * TS)
        horz[k // 2, half, half] = band(rolls[NB + k : NB + k + 1, :])
    loads[2].wait()

    row_iota = lax.broadcasted_iota(jnp.int32, (TS, TS), 0)
    col_iota = lax.broadcasted_iota(jnp.int32, (1, TS), 1)

    def pair(step, carry):
        two = jnp.concatenate([img[2 * step], img[2 * step + 1]], axis=1)
        bases = [table[128 + 2 * step + i] * (3 * NB) for i in range(2)]
        rho = [(row_iota + 8 * table[64 + 4 * step + 2 * i]).astype(F32) * (1.0 / WIN) for i in range(2)]
        gamma = [(col_iota + 8 * table[65 + 4 * step + 2 * i]).astype(F32) * (1.0 / WIN) for i in range(2)]
        for part in range(NB // 4):
            blurred = jnp.dot(
                vert[part * 4 * TS : (part + 1) * 4 * TS, :], two, preferred_element_type=F32
            )
            for kk in range(4):
                k = part * 4 + kk
                for i in range(2):
                    lm[i * TS : (i + 1) * TS, k * TS : (k + 1) * TS] = blurred[
                        kk * TS : (kk + 1) * TS, i * TS : (i + 1) * TS
                    ].astype(BF16)
        matched = [None, None]
        for kp in range(NB // 2):
            smooth = jnp.dot(lm[:, kp * 2 * TS : (kp + 1) * 2 * TS], horz[kp], preferred_element_type=F32)
            for kk in range(2):
                k = 2 * kp + kk
                for i in range(2):
                    a0 = coefs[bases[i] + k]
                    a1 = coefs[bases[i] + NB + k]
                    a2 = coefs[bases[i] + 2 * NB + k]
                    term = ((a0 + a1 * rho[i]) + a2 * gamma[i]) * smooth[
                        i * TS : (i + 1) * TS, kk * TS : (kk + 1) * TS
                    ]
                    matched[i] = term if matched[i] is None else matched[i] + term
        for i in range(2):
            tiles[2 * step + i] = matched[i].astype(BF16)
        return carry

    lax.fori_loop(0, NT // 2, pair, 0)

    def sort(j, carry):
        mat_out[j] = tiles[table[j]]
        return carry

    lax.fori_loop(0, NP * CAP, sort, 0)
    for c in own:
        c.wait()
    for c in copies:
        c.wait()


def front(table, coefs, rolls, meta, img, var, bad):
    dma = pltpu.SemaphoreType.DMA
    return pl.pallas_call(
        front_kernel,
        out_shape=(
            jax.ShapeDtypeStruct((NP, CAP, TS, TS), BF16),
            jax.ShapeDtypeStruct((NP * CAP, TS, TS), BF16),
            jax.ShapeDtypeStruct((NP, CAP, TS), jnp.int32),
        ),
        in_specs=[SMEM, SMEM, VMEM, ANY, ANY, ANY, ANY],
        out_specs=(ANY, VMEM, ANY),
        scratch_shapes=[
            pltpu.VMEM((NT, TS, TS), BF16),
            pltpu.VMEM((NT, TS, TS), BF16),
            pltpu.VMEM((NT, TS, TS), jnp.int32),
            pltpu.VMEM((NP * CAP, TS, TS), BF16),
            pltpu.VMEM((NT, TS, TS), BF16),
            pltpu.VMEM((NB * TS, TS), BF16),
            pltpu.VMEM((NB // 2, 2 * TS, 2 * TS), BF16),
            pltpu.VMEM((2 * TS, NB * TS), BF16),
            dma((3,)), dma((2,)), dma((2, NP)), dma((2, NP)),
        ],
        compiler_params=pltpu.CompilerParams(
            collective_id=0, has_side_effects=True, vmem_limit_bytes=40 * 2**20
        ),
        name="match_tiles",
    )(table, coefs, rolls, meta, img, var, bad)


def add_kernel(count, meta, *refs):
    tiles, (by_z, by_x, window) = refs[:count], refs[count:]
    source = pl.program_id(0)

    @pl.when(source == 0)
    def _():
        def clear(i, carry):
            window[i] = jnp.zeros((WIN, TS), F32)
            return carry

        lax.fori_loop(0, WIN // TS + 1, clear, 0)

    lane = lax.broadcasted_iota(jnp.int32, (TS, TS), 1)

    def add(s, carry):
        j = source * CAP + s

        @pl.when(meta[j, 2] > 0)
        def _():
            top = pl.multiple_of(meta[j, 0], 8)
            left = meta[j, 1]
            q = left // TS
            shift = lax.rem(left, TS)
            tile = tiles[0][s].astype(F32)
            for other in tiles[1:]:
                tile = tile * other[s].astype(F32)
            tile = pltpu.roll(tile, shift, 1)
            right_part = lane >= shift
            window[q, pl.ds(top, TS), :] += jnp.where(right_part, tile, 0.0)
            window[q + 1, pl.ds(top, TS), :] += jnp.where(right_part, 0.0, tile)

        return carry

    lax.fori_loop(0, CAP, add, 0)

    @pl.when(source == NP - 1)
    def _():
        def write(v, carry):
            x = v // NZ
            z = lax.rem(v, NZ)
            at = pl.multiple_of(v * ROWS, ROWS)
            for q in range(WIN // TS // 2):
                cols = slice(q * TS, (q + 1) * TS)
                by_z[z, x, :, cols] = window[q, pl.ds(at, ROWS), :].astype(BF16)
                by_x[x, z, :, cols] = window[q + WIN // TS // 2, pl.ds(at, ROWS), :].astype(BF16)
            return carry

        lax.fori_loop(0, NX * NZ, write, 0)


def add_tiles(meta, *tiles):
    block = pl.BlockSpec((CAP, TS, TS), lambda i: (i, 0, 0))
    return pl.pallas_call(
        functools.partial(add_kernel, len(tiles)),
        grid=(NP,),
        out_shape=(
            jax.ShapeDtypeStruct((NZ, NX, ROWS, HALF), BF16),
            jax.ShapeDtypeStruct((NX, NZ, ROWS, HALF), BF16),
        ),
        in_specs=[SMEM] + [block] * len(tiles),
        out_specs=(VMEM, VMEM),
        scratch_shapes=[pltpu.VMEM((WIN // TS + 1, WIN, TS), F32)],
        compiler_params=pltpu.CompilerParams(vmem_limit_bytes=40 * 2**20),
        name="add_tiles",
    )(meta, *(t.reshape(NP * CAP, TS, TS) for t in tiles))


class Ring:
    def __init__(self, n, me, device, src, send, recv, send_sem, recv_sem):
        self.n, self.me, self.device, self.src = n, me, device, src
        self.send, self.recv, self.send_sem, self.recv_sem = send, recv, send_sem, recv_sem
        self.copies = {}
        self.mid = src.shape[1] // 2

    def start(self, way, j):
        n, mid = self.n, self.mid
        to = lax.rem(self.me + (1 if way == 0 else n - 1), n)
        far = n // 2 - j
        owner = lax.rem(self.me + (far if way == 0 else n - far), n)
        own, other = (slice(0, mid), slice(mid, 2 * mid)) if way == 0 else (slice(mid, 2 * mid), slice(0, mid))
        if j == 0:
            src, dst = self.src.at[owner, own], self.recv.at[way, 0, own]
        else:
            got = self.recv.at[way, j - 1]
            self.copies[way, j - 1].wait_recv()
            dst, src = self.recv.at[way, j], self.send.at[way, j]
            block = self.src.at[owner]
            src[own] = (block[own].astype(F32) + got[own].astype(F32)).astype(BF16)
            if j == 1:
                src[other] = block[other]
            else:
                src[other] = (block[other].astype(F32) + got[other].astype(F32)).astype(BF16)
        copy = pltpu.make_async_remote_copy(
            src_ref=src,
            dst_ref=dst,
            send_sem=self.send_sem.at[way, j],
            recv_sem=self.recv_sem.at[way, j],
            device_id={"visit": self.device(to)},
            device_id_type=MESH,
        )
        copy.start()
        self.copies[way, j] = copy

    def total(self):
        last = self.n // 2 - 1
        for way in range(2):
            self.copies[way, last].wait_recv()
        return (
            self.src[self.me].astype(F32)
            + self.recv[0, last].astype(F32)
            + self.recv[1, last].astype(F32)
        )

    def finish(self):
        for copy in self.copies.values():
            copy.wait_send()


class Direct:
    def __init__(self, n, me, device, src, recv, send_sem, recv_sem):
        self.n, self.me, self.src, self.recv = n, me, src, recv
        self.copies = []
        for d in range(1, n):
            to = lax.rem(me + d, n)
            self.copies.append(
                pltpu.make_async_remote_copy(
                    src_ref=src.at[to],
                    dst_ref=recv.at[d],
                    send_sem=send_sem.at[d],
                    recv_sem=recv_sem.at[d],
                    device_id={"visit": device(to)},
                    device_id_type=MESH,
                )
            )
            self.copies[-1].start()

    def total(self):
        out = self.src[self.me].astype(F32)
        for d in range(1, self.n):
            self.copies[d - 1].wait_recv()
            out = out + self.recv[d].astype(F32)
        return out

    def finish(self):
        for copy in self.copies:
            copy.wait_send()


def place():
    me = lax.axis_index("visit")
    x, z = me // NZ, lax.rem(me, NZ)
    return x, z, lambda to: x * NZ + to, lambda to: to * NZ + z


def greet_groups():
    x, z, along_z, along_x = place()
    greet("visit", [along_z(lax.rem(z + d, NZ)) for d in range(1, NZ)])
    greet("visit", [along_x(lax.rem(x + d, NX)) for d in range(1, NX)])
    return NZ + NX - 2


def sum_groups(
    by_z, by_x, finish,
    z_send, z_recv, x_send, x_recv, z_mid, x_mid, z_got, x_got,
    zs_sem, zr_sem, xs_sem, xr_sem, zds_sem, zdr_sem, xds_sem, xdr_sem,
):
    x, z, along_z, along_x = place()
    ring_z = Ring(NZ, z, along_z, by_z, z_send, z_recv, zs_sem, zr_sem)
    ring_x = Ring(NX, x, along_x, by_x, x_send, x_recv, xs_sem, xr_sem)
    for j in range(2):
        for way in range(2):
            ring_z.start(way, j)
            ring_x.start(way, j)
    ring_z.start(0, 2)
    ring_z.start(1, 2)
    x_mid[...] = ring_x.total().astype(BF16)
    direct_z = Direct(NZ, z, along_z, x_mid, z_got, zds_sem, zdr_sem)
    ring_z.start(0, 3)
    ring_z.start(1, 3)
    z_mid[...] = ring_z.total().astype(BF16)
    direct_x = Direct(NX, x, along_x, z_mid, x_got, xds_sem, xdr_sem)
    finish(slice(HALF, WIN), direct_z.total())
    finish(slice(0, HALF), direct_x.total())
    for part in (ring_z, ring_x, direct_z, direct_x):
        part.finish()


def sum_scratch():
    z_block, x_block = (NX, ROWS, HALF), (NZ, ROWS, HALF)
    dma = pltpu.SemaphoreType.DMA
    return [
        pltpu.VMEM((2, NZ // 2) + z_block, BF16),
        pltpu.VMEM((2, NZ // 2) + z_block, BF16),
        pltpu.VMEM((2, NX // 2) + x_block, BF16),
        pltpu.VMEM((2, NX // 2) + x_block, BF16),
        pltpu.VMEM(z_block, BF16),
        pltpu.VMEM(x_block, BF16),
        pltpu.VMEM((NZ, ROWS, HALF), BF16),
        pltpu.VMEM((NX, ROWS, HALF), BF16),
        dma((2, NZ // 2)), dma((2, NZ // 2)), dma((2, NX // 2)), dma((2, NX // 2)),
        dma((NZ,)), dma((NZ,)), dma((NX,)), dma((NX,)),
    ]


def middle_kernel(mat, by_z, by_x, mat_out, depth, own_sem, send_sem, recv_sem, *scratch):
    me = lax.axis_index("patch")
    greet("patch", [lax.rem(me + d, NP) for d in range(1, NP)])
    number = greet_groups() + NP - 1
    pl.semaphore_wait(pltpu.get_barrier_semaphore(), number)
    copies = []
    for d in (4, 3, 5, 2, 6, 1, 7):
        there = lax.rem(me + d, NP)
        copies.append(
            pltpu.make_async_remote_copy(
                src_ref=mat.at[there],
                dst_ref=mat_out.at[me],
                send_sem=send_sem.at[d],
                recv_sem=recv_sem.at[d],
                device_id={"patch": there},
                device_id_type=MESH,
            )
        )
        copies[-1].start()
    own = pltpu.make_async_copy(mat.at[me], mat_out.at[me], own_sem)
    own.start()

    def finish(cols, total):
        depth[:, cols] = total

    sum_groups(by_z, by_x, finish, *scratch)
    own.wait()
    for c in copies:
        c.wait()


def middle(mat, by_z, by_x):
    dma = pltpu.SemaphoreType.DMA
    return pl.pallas_call(
        middle_kernel,
        out_shape=(
            jax.ShapeDtypeStruct((NP, CAP, TS, TS), BF16),
            jax.ShapeDtypeStruct((ROWS, WIN), F32),
        ),
        in_specs=[ANY, VMEM, VMEM],
        out_specs=(ANY, VMEM),
        scratch_shapes=[dma(()), dma((NP,)), dma((NP,))] + sum_scratch(),
        compiler_params=pltpu.CompilerParams(
            collective_id=1, has_side_effects=True, vmem_limit_bytes=40 * 2**20
        ),
        name="sum_depth",
    )(mat.reshape(NP, CAP, TS, TS), by_z, by_x)


def last_kernel(by_z, by_x, depth, coadd, *scratch):
    number = greet_groups()
    pl.semaphore_wait(pltpu.get_barrier_semaphore(), number)

    def finish(cols, total):
        coadd[:, cols] = total / jnp.maximum(depth[:, cols], 1.0)

    sum_groups(by_z, by_x, finish, *scratch)


def last(by_z, by_x, depth):
    return pl.pallas_call(
        last_kernel,
        out_shape=jax.ShapeDtypeStruct((ROWS, WIN), F32),
        in_specs=[VMEM, VMEM, VMEM],
        out_specs=VMEM,
        scratch_shapes=sum_scratch(),
        compiler_params=pltpu.CompilerParams(
            collective_id=2, has_side_effects=True, vmem_limit_bytes=40 * 2**20
        ),
        name="sum_numerator",
    )(by_z, by_x, depth)


def local(images, variances, bad_pixels, routes, offsets, tile_visits, coefficients, kernel_counts, taps):
    reach = taps.shape[2] // 2
    active = (lax.iota(jnp.int32, NB)[None, :] < kernel_counts[:, None])[:, None, :]
    coefs = jnp.where(active, coefficients.astype(F32), 0.0).reshape(-1)
    wide = taps.astype(F32)
    gap = jnp.zeros((NB, 2 * TS - taps.shape[2]), F32)
    vertical, horizontal = wide[:, 0], wide[:, 1, ::-1]
    rolls = jnp.concatenate(
        [jnp.concatenate([r[:, reach:], gap, r[:, :reach]], axis=1) for r in (vertical, horizontal)], axis=0
    )
    target = routes[:, 0]
    order = lax.iota(jnp.int32, NT)
    same = (target[:, None] == target[None, :]) & (order[None, :] < order[:, None])
    slot = target * CAP + jnp.sum(same.astype(jnp.int32), axis=1)
    chosen = slot[None, :] == lax.iota(jnp.int32, NP * CAP)[:, None]
    facts = jnp.stack([8 * offsets[:, 0], 8 * offsets[:, 1], jnp.ones_like(order), order], axis=0)
    slot_facts = jnp.sum(jnp.where(chosen[None], facts[:, None, :], 0), axis=2)
    table = jnp.concatenate([slot_facts[3], offsets.reshape(-1), tile_visits])
    meta = jnp.pad(slot_facts[:3].T, ((0, 0), (0, TS - 3))).reshape(NP, CAP, TS)

    wgt, mat, meta = front(table, coefs, rolls, meta, images, variances, bad_pixels)
    meta = meta.reshape(NP * CAP, TS)
    mat, depth = middle(mat, *add_tiles(meta, wgt))
    coadd = last(*add_tiles(meta, wgt, mat), depth)
    return coadd, depth


def solution(mesh):
    tiles = P(("patch", "visit"), None, None)
    return jax.shard_map(
        local,
        mesh=mesh,
        in_specs=(
            tiles, tiles, tiles,
            P(("patch", "visit"), None), P(("patch", "visit"), None), P(("patch", "visit")),
            P("visit", None, None), P("visit"), P(),
        ),
        out_specs=(P(("patch", "visit"), None), P(("patch", "visit"), None)),
        check_vma=False,
    )
```

time: 1470 us -> 123 us (0.08); the launches traced: 1450 us -> 122 us
  waiting for transfers between devices: 483 us -> 0 us
  local copies, waits for them, and re-layouts: 476 us -> 6.72 us
  loops' own time: 244 us -> 0 us
  matrix products: 120 us -> 0 us
  Pallas kernels: 0 us -> 110 us
  other arithmetic: 92 us -> 5.51 us
  starting transfers between devices: 16.4 us -> 0 us
    reduce_scatter x2 -> x0, waiting for transfers between devices: 463 us -> none  [the longest x1 239 us: local(): lax.psum_scatter(local_denom, 'visit', scatter_dimension=0, tiled=True)]
    dynamic_update_slice x128 -> x0, local copies, waits for them, and re-layouts: 393 us -> none  [the longest x64 198 us: add_slot(): lax.dynamic_update_slice(numer, lax.dynamic_slice(numer, (top, left), (ti...]
    another operation x2 -> x0, loops' own time: 244 us -> none  [the longest x1 243 us: local(): lax.fori_loop(0, slot_values.shape[0], add_slot, (empty, empty))]
    dot_general x54 -> x0, matrix products: 120 us -> none  [the longest x16 69.8 us: match_single(): terms = jnp.einsum('ck,kiv->civ', coefs, smoothed, precision=HIGHEST)]
    pallas_call x0 -> x5, Pallas kernels: none -> 110 us  [the longest x1 38 us: middle(): pl.pallas_call(middle_kernel, out_shape=(jax.ShapeDtypeStruct((NP, CAP, T...]
    add x65 -> x1, other arithmetic: 73.1 us -> 0.66 us  [local(): slot = target * CAP + jnp.sum(same.astype(jnp.int32), axis=1)]
    dynamic_slice x64 -> x0, local copies, waits for them, and re-layouts: 37.9 us -> none  [add_slot(): left = slot_corners[position, 1]]
    dot_general x16 -> x0, local copies, waits for them, and re-layouts: 21.7 us -> none  [match_single(): jnp.einsum('kij,jw->kiw', vertical, image, preferred_element_type=jnp.flo...]
  transfers between devices with their start and end apart: 5 -> 0, of which waited for: 3 -> 0; matrix products, arithmetic and copies ran while one was open for 12% -> 0% of each run, Pallas kernels for 0% -> 0%
where the time goes in v1:
time: 123 us; the launch traced here: 122 us
  Pallas kernels  110 us (89%)
  local copies, waits for them, and re-layouts  6.72 us (5%)
  other arithmetic  5.51 us (4%)
    pallas_call x1, Pallas kernels, middle(): pl.pallas_call(middle_kernel, out_shape=(jax.ShapeDtypeStruct((NP, CAP, T...  38 us
    pallas_call x1, Pallas kernels, last(): pl.pallas_call(last_kernel, out_shape=jax.ShapeDtypeStruct((ROWS, WIN), F...  32.3 us
    pallas_call x1, Pallas kernels, front(): pl.pallas_call(front_kernel, out_shape=(jax.ShapeDtypeStruct((NP, CAP, TS...  28.1 us
    pallas_call x2, Pallas kernels, add_tiles(): pl.pallas_call(functools.partial(add_kernel, len(tiles)), grid=(NP,), out...  11.1 us
    unnamed x10, local copies, waits for them, and re-layouts  6.21 us

profile of v1, /device:TPU:24, one launch (start us, length us, event | category | flops | bytes accessed | tf_op | source)
XLA Modules:
  0.0 122.5 jit_solution(10462432420002631727)
XLA Ops:
  0.6 0.7 iota_compare_fusion.2
  1.4 0.9 convert_reduce_fusion
  2.3 0.7 multiply_add_fusion
  3.0 0.8 multiply_bitcast_fusion.1
  3.8 0.7 convert_select_fusion
  4.5 0.1 reshape.98.coefs
  4.7 0.1 select_reduce_fusion
  4.8 0.7 copy_convert_fusion
  5.6 0.1 slice.44
  5.7 0.8 copy.19
  6.5 0.1 reshape.97
  6.6 0.7 pad_add_fusion.1.table
  7.4 0.1 maximum_maximum_fusion.rolls
  7.4 0.1 copy.23
  7.6 1.6 %copy-done = s32[32,128,128]{2,1,0:T(8,128)S(1)} copy-done((s32[32,128,128]{2,1,0:T(8,128)S(1)}, s32[32,128,128]{2,1,0:T(8,128)}, u32[]{:S(2)}) %copy-start) | copy-done | bytes 2097176
  9.1 1.2 copy-done.1
  10.4 1.2 copy-done.2
  11.6 28.1 %match_tiles.1 = (bf16[8,8,128,128]{3,2,1,0:T(8,128)(2,1)S(1)}, bf16[64,128,128]{2,1,0:T(8,128)(2,1)S(1)}, s32[8,8,128]{2,1,0:T(8,128)S(1)}) custom-call(s32[160]{0:T(256)S(1)} %pad_add_fusion.1.table, f32[96]{0:T(128)S(1)} %reshape.98.coefs, f32[32,256]{1,0:T(8,128)S(1)} %maximum_maximum_fusion.rolls, s32[8,8,128]{2,1,0:T(8,128)S(1)} %pad_bitcast_fusion.meta, ...), custom_call_target="tpu_custom_call" | custom-call | tf_op jit(solution)/shard_map/match_tiles/pallas_call | solution.py:144
  39.7 5.5 %add_tiles.2 = (bf16[8,4,32,512]{3,2,1,0:T(8,128)(2,1)S(1)}, bf16[4,8,32,512]{3,2,1,0:T(8,128)(2,1)S(1)}) custom-call(s32[64,128]{1,0:T(8,128)S(1)} %bitcast.26, bf16[64,128,128]{2,1,0:T(8,128)(2,1)S(1)} %bitcast.22), custom_call_target="tpu_custom_call" | custom-call | tf_op jit(solution)/shard_map/add_tiles/pallas_call | solution.py:223
  45.2 38.0 %sum_depth.1 = (bf16[8,8,128,128]{3,2,1,0:T(8,128)(2,1)S(1)}, f32[32,1024]{1,0:T(8,128)S(1)}) custom-call(bf16[8,8,128,128]{3,2,1,0:T(8,128)(2,1)S(1)} %bitcast.24, bf16[8,4,32,512]{3,2,1,0:T(8,128)(2,1)S(1)} %get-tuple-element.14.by_z, bf16[4,8,32,512]{3,2,1,0:T(8,128)(2,1)S(1)} %get-tuple-element.15.by_x), custom_call_target="tpu_custom_call" | custom-call | tf_op jit(solution)/shard_map/sum_depth/pallas_call | solution.py:408
  83.2 5.6 %add_tiles.3 = (bf16[8,4,32,512]{3,2,1,0:T(8,128)(2,1)S(1)}, bf16[4,8,32,512]{3,2,1,0:T(8,128)(2,1)S(1)}) custom-call(s32[64,128]{1,0:T(8,128)S(1)} %bitcast.27, bf16[64,128,128]{2,1,0:T(8,128)(2,1)S(1)} %bitcast.23, bf16[64,128,128]{2,1,0:T(8,128)(2,1)S(1)} %bitcast.25), custom_call_target="tpu_custom_call" | custom-call | tf_op jit(solution)/shard_map/add_tiles/pallas_call | solution.py:223
  88.8 32.3 %sum_numerator.1 = f32[32,1024]{1,0:T(8,128)S(1)} custom-call(bf16[8,4,32,512]{3,2,1,0:T(8,128)(2,1)S(1)} %get-tuple-element.17.by_z, bf16[4,8,32,512]{3,2,1,0:T(8,128)(2,1)S(1)} %get-tuple-element.18.by_x, f32[32,1024]{1,0:T(8,128)S(1)} %get-tuple-element.27.depth), custom_call_target="tpu_custom_call" | custom-call | tf_op jit(solution)/shard_map/sum_numerator/pallas_call | solution.py:435
  121.1 0.7 copy.27
  121.8 0.7 copy.28
  (15 shorter events, 0.4 us)
Async XLA Ops:
  7.5 1.6 %copy-start = (s32[32,128,128]{2,1,0:T(8,128)S(1)}, s32[32,128,128]{2,1,0:T(8,128)}, u32[]{:S(2)}) copy-start(s32[32,128,128]{2,1,0:T(8,128)} %bad_in.1) | copy-start | bytes 6291460
  9.1 1.2 %copy-start.1 = (bf16[32,128,128]{2,1,0:T(8,128)(2,1)S(1)}, bf16[32,128,128]{2,1,0:T(8,128)(2,1)}, u32[]{:S(2)}) copy-start(bf16[32,128,128]{2,1,0:T(8,128)(2,1)} %img_in.1) | copy-start | bytes 3145732
  10.4 1.2 %copy-start.2 = (bf16[32,128,128]{2,1,0:T(8,128)(2,1)S(1)}, bf16[32,128,128]{2,1,0:T(8,128)(2,1)}, u32[]{:S(2)}) copy-start(bf16[32,128,128]{2,1,0:T(8,128)(2,1)} %var_in.1) | copy-start | bytes 3145732

commit v2 on v0

v2 whole, which is shorter than its diff:
```python
import jax
import jax.numpy as jnp
from jax import lax
from jax.experimental import pallas as pl
from jax.experimental.pallas import tpu as pltpu
from jax.sharding import PartitionSpec as P

TS = 128
WIN = 1024
CAP = 8
NB = 16
NT = 32
NP = 8
NA = 4
NZ = 8
SIDE = 16
STEPS = ((2, 0), (2, 1), (1, 0), (3, 0), (1, 1), (3, 1), (0, 1), (0, 0))
BLOCKS = (4, 3, 5, 2, 6, 1, 7, 0)
PIECES = (slice(0, 1), slice(1, 3), slice(3, 5), slice(5, 7), slice(7, 8))
FAR_PIECES = (slice(0, 3), slice(3, 8))
MESH = pl.DeviceIdType.MESH
BF16 = jnp.bfloat16
F32 = jnp.float32
VMEM = pl.BlockSpec(memory_space=pltpu.VMEM)
SMEM = pl.BlockSpec(memory_space=pltpu.SMEM)
HBM = pl.BlockSpec(memory_space=pltpu.HBM)
ANY = pl.BlockSpec(memory_space=pl.ANY)


def place():
    patch, visit = lax.axis_index("patch"), lax.axis_index("visit")
    return visit // NZ, patch // 2, lax.rem(visit, NZ), lax.rem(patch, 2)


def patch_at(ring, core, step):
    return lax.rem(ring + step[0], NA) * 2 + lax.rem(core + step[1], 2)


def signal(device):
    pl.semaphore_signal(pltpu.get_barrier_semaphore(), inc=1, device_id=device, device_id_type=MESH)


def wait(number):
    pl.semaphore_wait(pltpu.get_barrier_semaphore(), number)


def send(src, dst, send_sem, recv_sem, device):
    copy = pltpu.make_async_remote_copy(
        src_ref=src, dst_ref=dst, send_sem=send_sem, recv_sem=recv_sem, device_id=device, device_id_type=MESH
    )
    copy.start()
    return copy


def slot_kernel(routes, offsets, table, meta, count, first):
    _, y, _, core = place()
    lane = lax.broadcasted_iota(jnp.int32, (1, TS), 1)
    meta[...] = jnp.zeros_like(meta)
    for j in range(NP * CAP):
        table[j] = 0
    for p in range(NP):
        count[p] = 0

    def tally(t, carry):
        p = routes[0, t]
        count[p] = count[p] + 1
        return carry

    lax.fori_loop(0, NT, tally, 0)
    begin = 0
    for step in STEPS:
        p = patch_at(y, core, step)
        first[p] = begin
        begin = begin + count[p]
        count[p] = 0

    def fill(t, carry):
        p = routes[0, t]
        s = count[p]
        count[p] = s + 1
        i = first[p] + s
        table[NP * CAP + i] = t
        table[p * CAP + s] = i
        facts = jnp.where(lane == 1, 8 * offsets[1, t], jnp.where(lane == 2, 1, 0))
        meta[p, pl.ds(s, 1), :] = jnp.where(lane == 0, 8 * offsets[0, t], facts)
        return carry

    lax.fori_loop(0, NT, fill, 0)


def slots(routes, offsets):
    return pl.pallas_call(
        slot_kernel,
        out_shape=(
            jax.ShapeDtypeStruct((NP * CAP + NT,), jnp.int32),
            jax.ShapeDtypeStruct((NP, CAP, TS), jnp.int32),
        ),
        in_specs=[SMEM, SMEM],
        out_specs=(SMEM, VMEM),
        scratch_shapes=[pltpu.SMEM((NP,), jnp.int32), pltpu.SMEM((NP,), jnp.int32)],
        name="slots",
    )(routes, offsets)


def band(row):
    wide = jnp.broadcast_to(row, (TS, 2 * TS))
    return pltpu.roll(wide, 0, 1, stride=1, stride_axis=0)[:, :TS].astype(BF16)


def match_kernel(
    table, offsets, visits, counts, coefs, taps, meta, img_in, var_in, bad_in, wgt_out, num_out, facts_out,
    img, var, bad, weights, products, wslots, nslots, vert, horz, lm, rows, in_sem, own_sem, send_sem, recv_sem,
):
    x, y, z, core = place()
    loads = [
        pltpu.make_async_copy(src, dst, in_sem.at[i])
        for i, (src, dst) in enumerate(((var_in, var), (bad_in, bad), (img_in, img)))
    ]
    for load in loads:
        load.start()

    def along_x(step):
        return {"patch": y * 2 + lax.rem(core + step[1], 2), "visit": lax.rem(x + step[0], NA) * NZ + z}

    def along_y(step):
        return {"patch": patch_at(y, core, step)}

    for step in STEPS[:-1]:
        signal(along_x(step))
        signal(along_y(step))

    loads[0].wait()
    loads[1].wait()

    def weigh(i, carry):
        t = table[NP * CAP + i]
        weights[i] = jnp.where(bad[t] == 0, 1.0 / var[t].astype(F32), 0.0).astype(BF16)
        return carry

    lax.fori_loop(0, NT, weigh, 0)
    copies = []

    def to_patch(kind, r):
        source, made, out = ((weights, wslots, wgt_out), (products, nslots, num_out))[kind]
        ring = x if kind == 0 else y
        there, here = patch_at(ring, core, STEPS[r]), ring * 2 + core

        def sort(j, carry):
            made[j] = source[table[j]]
            return carry

        lax.fori_loop(there * CAP, there * CAP + CAP, sort, 0)
        pairs = ((meta.at[there], facts_out.at[kind, here]), (made.at[pl.ds(there * CAP, CAP)], out.at[here]))
        for i, (src, dst) in enumerate(pairs):
            if r == NP - 1:
                copy = pltpu.make_async_copy(src, dst, own_sem.at[kind, i])
                copy.start()
            else:
                device = along_x(STEPS[r]) if kind == 0 else along_y(STEPS[r])
                copy = send(src, dst, send_sem.at[kind, i, r], recv_sem.at[kind, i, r], device)
            copies.append(copy)

    wait(2 * (NP - 1))
    for r in range(NP):
        to_patch(0, r)

    span = taps.shape[2]
    tap = lax.broadcasted_iota(jnp.int32, (span, 2 * TS), 0) - span // 2
    spot = lax.broadcasted_iota(jnp.int32, (span, 2 * TS), 1)
    spot = jnp.where(spot < TS, spot, spot - 2 * TS)
    down = jnp.dot(taps[:, 0, :], (spot == tap).astype(BF16), preferred_element_type=F32)
    across = jnp.dot(taps[:, 1, :], (spot == -tap).astype(BF16), preferred_element_type=F32)
    horz[...] = jnp.zeros_like(horz)
    for k in range(NB):
        vert[k * TS : (k + 1) * TS, :] = band(down[k : k + 1, :])
        half = slice((k % 2) * TS, (k % 2 + 1) * TS)
        horz[k // 2, half, half] = band(across[k : k + 1, :])
    level = lax.broadcasted_iota(jnp.int32, (NB, NB), 0)
    column = lax.broadcasted_iota(jnp.int32, (NB, NB), 1)
    for v in range(2):
        for c in range(3):
            used = (level == column) & (level < counts[v])
            diagonal = jnp.where(used, coefs[c, v : v + 1, :].astype(F32), 0.0).astype(BF16)
            rows[v, c] = jnp.dot(diagonal, jnp.ones((NB, TS), BF16), preferred_element_type=F32)
    loads[2].wait()

    row_iota = lax.broadcasted_iota(jnp.int32, (TS, TS), 0)
    col_iota = lax.broadcasted_iota(jnp.int32, (1, TS), 1)

    def pair(step, carry):
        ids = [table[NP * CAP + 2 * step + i] for i in range(2)]
        two = jnp.concatenate([img[ids[0]], img[ids[1]]], axis=1)
        own_visit = [visits[t] for t in ids]
        rho = [(row_iota + 8 * offsets[0, t]).astype(F32) * (1.0 / WIN) for t in ids]
        gamma = [(col_iota + 8 * offsets[1, t]).astype(F32) * (1.0 / WIN) for t in ids]
        for part in range(NB // 4):
            blurred = jnp.dot(
                vert[part * 4 * TS : (part + 1) * 4 * TS, :], two, preferred_element_type=F32
            )
            for kk in range(4):
                k = part * 4 + kk
                for i in range(2):
                    lm[i * TS : (i + 1) * TS, k * TS : (k + 1) * TS] = blurred[
                        kk * TS : (kk + 1) * TS, i * TS : (i + 1) * TS
                    ].astype(BF16)
        matched = [None, None]
        for kp in range(NB // 2):
            smooth = jnp.dot(lm[:, kp * 2 * TS : (kp + 1) * 2 * TS], horz[kp], preferred_element_type=F32)
            for kk in range(2):
                k = 2 * kp + kk
                for i in range(2):
                    a0, a1, a2 = (rows[own_visit[i], c, k : k + 1, :] for c in range(3))
                    term = (a1 * rho[i] + (a0 + a2 * gamma[i])) * smooth[
                        i * TS : (i + 1) * TS, kk * TS : (kk + 1) * TS
                    ]
                    matched[i] = term if matched[i] is None else matched[i] + term
        for i in range(2):
            weight = weights[2 * step + i].astype(F32)
            products[2 * step + i] = (weight * matched[i].astype(BF16).astype(F32)).astype(BF16)
        return carry

    for r in range(NT // CAP):
        lax.fori_loop(r * CAP // 2, (r + 1) * CAP // 2, pair, 0)
        if r < NT // CAP - 1:
            to_patch(1, r)
    for r in range(NT // CAP - 1, NP):
        to_patch(1, r)
    for copy in copies:
        copy.wait()


def match(*operands):
    dma = pltpu.SemaphoreType.DMA
    got = jax.ShapeDtypeStruct((NP, CAP, TS, TS), BF16)
    facts = jax.ShapeDtypeStruct((2, NP, CAP, TS), jnp.int32)
    return pl.pallas_call(
        match_kernel,
        out_shape=(got, got, facts),
        in_specs=[SMEM, SMEM, SMEM, SMEM, VMEM, VMEM, VMEM, HBM, HBM, HBM],
        out_specs=(ANY, ANY, ANY),
        scratch_shapes=[
            pltpu.VMEM((NT, TS, TS), BF16),
            pltpu.VMEM((NT, TS, TS), BF16),
            pltpu.VMEM((NT, TS, TS), jnp.int32),
            pltpu.VMEM((NT, TS, TS), BF16),
            pltpu.VMEM((NT, TS, TS), BF16),
            pltpu.VMEM((NP * CAP, TS, TS), BF16),
            pltpu.VMEM((NP * CAP, TS, TS), BF16),
            pltpu.VMEM((NB * TS, TS), BF16),
            pltpu.VMEM((NB // 2, 2 * TS, 2 * TS), BF16),
            pltpu.VMEM((2 * TS, NB * TS), BF16),
            pltpu.VMEM((2, 3, NB, TS), F32),
            dma((3,)), dma((2, 2)), dma((2, 2, NP)), dma((2, 2, NP)),
        ],
        compiler_params=pltpu.CompilerParams(
            collective_id=0, has_side_effects=True, vmem_limit_bytes=54 * 2**20
        ),
        name="match_tiles",
    )(*operands)


def add_kernel(facts, wgt, num, wgt_sum, num_sum, wgt_window, num_window):
    source = pl.program_id(0)
    planes = ((0, wgt, wgt_sum, wgt_window), (1, num, num_sum, num_window))

    @pl.when(source == 0)
    def _():
        def clear(i, carry):
            for plane in planes:
                plane[3][i] = jnp.zeros((WIN, TS), F32)
            return carry

        lax.fori_loop(0, WIN // TS + 1, clear, 0)

    lane = lax.broadcasted_iota(jnp.int32, (TS, TS), 1)
    for kind, tiles, _, window in planes:
        work = []
        for s in range(CAP):
            j = source * CAP + s
            used = facts[kind, j, 2]
            top = pl.multiple_of(facts[kind, j, 0], 8)
            left = facts[kind, j, 1]
            shift = lax.rem(left, TS)
            tile = pltpu.roll(tiles[s].astype(F32), shift, 1)
            here = lane >= jnp.where(used > 0, shift, TS)
            there = lane < jnp.where(used > 0, shift, 0)
            work.append((left // TS, top, tile, here, there))
        for q, top, tile, here, there in work:
            window[q, pl.ds(top, TS), :] += jnp.where(here, tile, 0.0)
            window[q + 1, pl.ds(top, TS), :] += jnp.where(there, tile, 0.0)

    @pl.when(source == NP - 1)
    def _():
        _, _, z, _ = place()

        def write(a, carry):
            for i, k in enumerate(BLOCKS):
                v = a * NZ + lax.rem(z + k, NZ)
                for half in range(2):
                    at = pl.multiple_of((2 * v + half) * SIDE, SIDE)
                    for _, _, out, window in planes:
                        for q in range(WIN // TS):
                            out[a, i, half, :, q * TS : (q + 1) * TS] = window[q, pl.ds(at, SIDE), :].astype(BF16)
            return carry

        lax.fori_loop(0, NA, write, 0)


def add_tiles(wgt, num, facts):
    block = pl.BlockSpec((CAP, TS, TS), lambda i: (i, 0, 0))
    out = jax.ShapeDtypeStruct((NA, NZ, 2, SIDE, WIN), BF16)
    tiles = [t.reshape(NP * CAP, TS, TS) for t in (wgt, num)]
    return pl.pallas_call(
        add_kernel,
        grid=(NP,),
        out_shape=(out, out),
        in_specs=[SMEM, block, block],
        out_specs=(VMEM, VMEM),
        scratch_shapes=[pltpu.VMEM((WIN // TS + 1, WIN, TS), F32)] * 2,
        compiler_params=pltpu.CompilerParams(vmem_limit_bytes=40 * 2**20),
        name="add_tiles",
    )(facts.reshape(2, NP * CAP, TS), *tiles)


class Plane:
    def __init__(self, a, z, along_a, along_z, src, a_recv, a_send, mid, z_recv, z_send, as_sem, ar_sem, zs_sem, zr_sem):
        self.a, self.z, self.along_a, self.along_z, self.src = a, z, along_a, along_z, src
        self.a_recv, self.a_send, self.mid, self.z_recv, self.z_send = a_recv, a_send, mid, z_recv, z_send
        self.as_sem, self.ar_sem, self.zs_sem, self.zr_sem = as_sem, ar_sem, zs_sem, zr_sem
        self.copies = {}

    def pass_on(self, name, way, step, i, src, dst):
        to = self.along_a(lax.rem(self.a + (1, NA - 1)[way], NA))
        sems = self.as_sem.at[way, step, i], self.ar_sem.at[way, step, i]
        self.copies[name, way, i] = send(src, dst, *sems, to)

    def first(self, i):
        piece = FAR_PIECES[i]
        for way in range(2):
            there = self.src.at[lax.rem(self.a + 2, NA), piece, way]
            self.pass_on("far", way, 0, i, there, self.a_recv.at[way, 0, piece])

    def second(self, i):
        piece = PIECES[i]
        for f, far in enumerate(FAR_PIECES):
            if far.start == piece.start:
                for way in range(2):
                    self.copies["far", way, f].wait_recv()
        for way in range(2):
            to = lax.rem(self.a + (1, NA - 1)[way], NA)
            mine = self.src[to, piece, way].astype(F32)
            self.a_send[way, piece] = (mine + self.a_recv[way, 0, piece].astype(F32)).astype(BF16)
            self.pass_on("sum", way, 2, i, self.a_send.at[way, piece], self.a_recv.at[way, 2, piece])
            self.pass_on("raw", way, 1, i, self.src.at[to, piece, 1 - way], self.a_recv.at[way, 1, piece])

    def ready(self, i):
        for way in range(2):
            self.copies["raw", way, i].wait_recv()
            self.copies["sum", way, i].wait_recv()

    def ring_sum(self, at):
        return [
            self.src[self.a, at, half].astype(F32)
            + self.a_recv[half, 2, at].astype(F32)
            + self.a_recv[1 - half, 1, at].astype(F32)
            for half in range(2)
        ]

    def keep(self, at):
        for half, value in enumerate(self.ring_sum(at)):
            self.mid[at, half] = value.astype(BF16)

    def along(self, j):
        for way in range(2):
            at = BLOCKS.index(4 - j if way == 0 else 4 + j)
            to = self.along_z(lax.rem(self.z + (1 if way == 0 else NZ - 1), NZ))
            if j == 0:
                src, dst = self.mid.at[at, way], self.z_recv.at[way, 0, way]
            else:
                src, dst = self.z_send.at[way, j - 1], self.z_recv.at[way, j]
                self.copies["z", way, j - 1].wait_recv()
                block, got = self.mid.at[at], self.z_recv.at[way, j - 1]
                src[way] = (block[way].astype(F32) + got[way].astype(F32)).astype(BF16)
                if j == 1:
                    src[1 - way] = block[1 - way]
                else:
                    src[1 - way] = (block[1 - way].astype(F32) + got[1 - way].astype(F32)).astype(BF16)
            self.copies["z", way, j] = send(src, dst, self.zs_sem.at[way, j], self.zr_sem.at[way, j], to)

    def total(self):
        out = self.ring_sum(NZ - 1)
        for way in range(2):
            self.copies["z", way, 3].wait_recv()
            out = [value + self.z_recv[way, 3, half].astype(F32) for half, value in enumerate(out)]
        return jnp.concatenate(out, axis=0)

    def finish(self):
        for copy in self.copies.values():
            copy.wait_send()


PLANE_SCRATCH = 9


def plane_scratch():
    block = (2, SIDE, WIN)
    dma = pltpu.SemaphoreType.DMA
    return [
        pltpu.VMEM((2, 3, NZ, SIDE, WIN), BF16),
        pltpu.VMEM((2, NZ, SIDE, WIN), BF16),
        pltpu.VMEM((NZ,) + block, BF16),
        pltpu.VMEM((2, NZ // 2) + block, BF16),
        pltpu.VMEM((2, NZ // 2 - 1) + block, BF16),
        dma((2, 3, len(PIECES))), dma((2, 3, len(PIECES))), dma((2, NZ // 2)), dma((2, NZ // 2)),
    ]


def sum_kernel(wgt, num, coadd, depth, *scratch):
    x, y, z, core = place()
    along_x = lambda to: {"visit": to * NZ + z}
    along_y = lambda to: {"patch": to * 2 + core}
    along_z = lambda to: {"visit": x * NZ + to}
    swapped = {"patch": x * 2 + core, "visit": y * NZ + z}
    moved, swap_send, swap_recv = scratch[2 * PLANE_SCRATCH :]

    for to in (1, NA - 1):
        signal(along_x(lax.rem(x + to, NA)))
        signal(along_y(lax.rem(y + to, NA)))
    for to in (1, NZ - 1):
        signal(along_z(lax.rem(z + to, NZ)))

    @pl.when(x != y)
    def _():
        signal(swapped)
        wait(7)

    @pl.when(x == y)
    def _():
        wait(6)

    planes = (
        Plane(y, z, along_y, along_z, wgt, *scratch[:PLANE_SCRATCH]),
        Plane(x, z, along_x, along_z, num, *scratch[PLANE_SCRATCH : 2 * PLANE_SCRATCH]),
    )
    for i in range(len(FAR_PIECES)):
        for plane in planes:
            plane.first(i)
    for i in range(len(PIECES)):
        for plane in planes:
            plane.second(i)
    for i in range(len(PIECES)):
        for plane in planes:
            plane.ready(i)
            for at in range(NZ - 1)[PIECES[i]]:
                plane.keep(at)
        if i < NZ // 2:
            for plane in planes:
                plane.along(i)
    total = planes[0].total()

    @pl.when(x != y)
    def _():
        moved[...] = total
        send(moved, depth, swap_send, swap_recv, swapped).wait()

    @pl.when(x == y)
    def _():
        depth[...] = total

    coadd[...] = planes[1].total() / jnp.maximum(depth[...], 1.0)
    for plane in planes:
        plane.finish()


def sum_windows(wgt, num):
    out = jax.ShapeDtypeStruct((2 * SIDE, WIN), F32)
    return pl.pallas_call(
        sum_kernel,
        out_shape=(out, out),
        in_specs=[VMEM, VMEM],
        out_specs=(VMEM, VMEM),
        scratch_shapes=plane_scratch()
        + plane_scratch()
        + [pltpu.VMEM((2 * SIDE, WIN), F32), pltpu.SemaphoreType.DMA, pltpu.SemaphoreType.DMA],
        compiler_params=pltpu.CompilerParams(
            collective_id=1, has_side_effects=True, vmem_limit_bytes=40 * 2**20
        ),
        name="sum_windows",
    )(wgt, num)


def local(images, variances, bad_pixels, routes, offsets, tile_visits, coefficients, kernel_counts, taps):
    routes, offsets, coefficients = routes.T, offsets.T, coefficients.transpose(1, 0, 2)
    table, meta = slots(routes, offsets)
    got = match(
        table, offsets, tile_visits, kernel_counts, coefficients, taps, meta, images, variances, bad_pixels
    )
    return sum_windows(*add_tiles(*got))


def solution(mesh):
    tiles = P(("patch", "visit"), None, None)
    return jax.shard_map(
        local,
        mesh=mesh,
        in_specs=(
            tiles, tiles, tiles,
            P(("patch", "visit"), None), P(("patch", "visit"), None), P(("patch", "visit")),
            P("visit", None, None), P("visit"), P(),
        ),
        out_specs=(P(("patch", "visit"), None), P(("patch", "visit"), None)),
        check_vma=False,
    )
```

time: 1470 us -> 88.9 us (0.06); the launches traced: 1450 us -> 87.9 us
  waiting for transfers between devices: 483 us -> 0 us
  local copies, waits for them, and re-layouts: 476 us -> 5.33 us
  loops' own time: 244 us -> 0 us
  matrix products: 120 us -> 0 us
  other arithmetic: 92 us -> 0 us
  Pallas kernels: 0 us -> 81.9 us
  starting transfers between devices: 16.4 us -> 0 us
    reduce_scatter x2 -> x0, waiting for transfers between devices: 463 us -> none  [the longest x1 239 us: local(): lax.psum_scatter(local_denom, 'visit', scatter_dimension=0, tiled=True)]
    dynamic_update_slice x128 -> x0, local copies, waits for them, and re-layouts: 393 us -> none  [the longest x64 198 us: add_slot(): lax.dynamic_update_slice(numer, lax.dynamic_slice(numer, (top, left), (ti...]
    another operation x2 -> x0, loops' own time: 244 us -> none  [the longest x1 243 us: local(): lax.fori_loop(0, slot_values.shape[0], add_slot, (empty, empty))]
    dot_general x54 -> x0, matrix products: 120 us -> none  [the longest x16 69.8 us: match_single(): terms = jnp.einsum('ck,kiv->civ', coefs, smoothed, precision=HIGHEST)]
    pallas_call x0 -> x4, Pallas kernels: none -> 81.9 us  [the longest x1 40.1 us: sum_windows(): pl.pallas_call(sum_kernel, out_shape=(out, out), in_specs=[VMEM, VMEM], o...]
    add x65 -> x0, other arithmetic: 73.1 us -> none  [the longest x64 72.4 us: add_slot(): lax.dynamic_slice(denom, (top, left), (tile_side, tile_side)) + weight_tile]
    dynamic_slice x64 -> x0, local copies, waits for them, and re-layouts: 37.9 us -> none  [add_slot(): left = slot_corners[position, 1]]
    dot_general x16 -> x0, local copies, waits for them, and re-layouts: 21.7 us -> none  [match_single(): jnp.einsum('kij,jw->kiw', vertical, image, preferred_element_type=jnp.flo...]
  transfers between devices with their start and end apart: 5 -> 0, of which waited for: 3 -> 0; matrix products, arithmetic and copies ran while one was open for 12% -> 0% of each run, Pallas kernels for 0% -> 0%
where the time goes in v2:
time: 88.9 us; the launch traced here: 87.9 us
  Pallas kernels  81.9 us (92%)
  local copies, waits for them, and re-layouts  5.33 us (6%)
    pallas_call x1, Pallas kernels, sum_windows(): pl.pallas_call(sum_kernel, out_shape=(out, out), in_specs=[VMEM, VMEM], o...  40.1 us
    pallas_call x1, Pallas kernels, match(): pl.pallas_call(match_kernel, out_shape=(got, got, facts), in_specs=[SMEM,...  34.4 us
    unnamed x8, local copies, waits for them, and re-layouts  5.33 us
    pallas_call x1, Pallas kernels, add_tiles(): pl.pallas_call(add_kernel, grid=(NP,), out_shape=(out, out), in_specs=[SM...  5.32 us
    pallas_call x1, Pallas kernels, slots(): pl.pallas_call(slot_kernel, out_shape=(jax.ShapeDtypeStruct((NP * CAP + N...  2.09 us

profile of v2, /device:TPU:24, one launch (start us, length us, event | category | flops | bytes accessed | tf_op | source)
XLA Modules:
  0.0 87.9 jit_solution(9612332432379386513)
XLA Ops:
  0.6 2.1 %slots.1 = (s32[96]{0:T(128)}, s32[8,8,128]{2,1,0:T(8,128)}) custom-call(s32[1,32]{1,0:T(1,128)} %bitcast.12, s32[2,32]{1,0:T(2,128)} %bitcast.10), custom_call_target="tpu_custom_call" | custom-call | tf_op jit(solution)/shard_map/slots/pallas_call | solution.py:92
  2.7 34.4 %match_tiles.1 = (bf16[8,8,128,128]{3,2,1,0:T(8,128)(2,1)}, bf16[8,8,128,128]{3,2,1,0:T(8,128)(2,1)}, s32[2,8,8,128]{3,2,1,0:T(8,128)}) custom-call(s32[96]{0:T(128)} %get-tuple-element.9.table, s32[2,32]{1,0:T(2,128)} %bitcast.11, s32[32]{0:T(128)} %visits.1, s32[2]{0:T(128)} %counts.1, bf16[3,2,16]{2,1,0:T(2,128)(2,1)} %bitcast.9, ...), custom_call_target="tpu_custom_call" | custom-call | tf_op jit(solution)/shard_map/match_tiles/pallas_call | solution.py:236
  37.1 0.0 copy-start
  37.1 1.6 %copy-done = bf16[8,8,128,128]{3,2,1,0:T(8,128)(2,1)S(1)} copy-done((bf16[8,8,128,128]{3,2,1,0:T(8,128)(2,1)S(1)}, bf16[8,8,128,128]{3,2,1,0:T(8,128)(2,1)}, u32[]{:S(2)}) %copy-start) | copy-done | bytes 2097176
  38.7 0.0 copy-start.1
  38.7 1.6 %copy-done.1 = bf16[8,8,128,128]{3,2,1,0:T(8,128)(2,1)S(1)} copy-done((bf16[8,8,128,128]{3,2,1,0:T(8,128)(2,1)S(1)}, bf16[8,8,128,128]{3,2,1,0:T(8,128)(2,1)}, u32[]{:S(2)}) %copy-start.1) | copy-done | bytes 2097176
  40.3 0.0 copy-start.2
  40.3 0.8 copy-done.2
  41.1 5.3 %add_tiles.1 = (bf16[4,8,2,16,1024]{4,3,2,1,0:T(8,128)(2,1)S(1)}, bf16[4,8,2,16,1024]{4,3,2,1,0:T(8,128)(2,1)S(1)}) custom-call(s32[2,64,128]{2,1,0:T(8,128)S(1)} %bitcast.8, bf16[64,128,128]{2,1,0:T(8,128)(2,1)S(1)} %bitcast.6, bf16[64,128,128]{2,1,0:T(8,128)(2,1)S(1)} %bitcast.7), custom_call_target="tpu_custom_call" | custom-call | tf_op jit(solution)/shard_map/add_tiles/pallas_call | solution.py:313
  46.5 40.1 %sum_windows.1 = (f32[32,1024]{1,0:T(8,128)S(1)}, f32[32,1024]{1,0:T(8,128)S(1)}) custom-call(bf16[4,8,2,16,1024]{4,3,2,1,0:T(8,128)(2,1)S(1)} %get-tuple-element.14.wgt, bf16[4,8,2,16,1024]{4,3,2,1,0:T(8,128)(2,1)S(1)} %get-tuple-element.15.num), custom_call_target="tpu_custom_call" | custom-call | tf_op jit(solution)/shard_map/sum_windows/pallas_call | solution.py:477
  86.6 0.7 copy.13
  87.2 0.7 copy.14
Async XLA Ops:
  37.1 1.6 %copy-start = (bf16[8,8,128,128]{3,2,1,0:T(8,128)(2,1)S(1)}, bf16[8,8,128,128]{3,2,1,0:T(8,128)(2,1)}, u32[]{:S(2)}) copy-start(bf16[8,8,128,128]{3,2,1,0:T(8,128)(2,1)} %get-tuple-element.12) | copy-start | bytes 6291460
  38.7 1.6 %copy-start.1 = (bf16[8,8,128,128]{3,2,1,0:T(8,128)(2,1)S(1)}, bf16[8,8,128,128]{3,2,1,0:T(8,128)(2,1)}, u32[]{:S(2)}) copy-start(bf16[8,8,128,128]{3,2,1,0:T(8,128)(2,1)} %get-tuple-element.13) | copy-start | bytes 6291460
  40.3 0.8 copy-start.2

commit v3 on v2

--- a/solution.py
+++ b/solution.py
@@ -129,41 +129,6 @@
         signal(along_x(step))
         signal(along_y(step))
 
-    loads[0].wait()
-    loads[1].wait()
-
-    def weigh(i, carry):
-        t = table[NP * CAP + i]
-        weights[i] = jnp.where(bad[t] == 0, 1.0 / var[t].astype(F32), 0.0).astype(BF16)
-        return carry
-
-    lax.fori_loop(0, NT, weigh, 0)
-    copies = []
-
-    def to_patch(kind, r):
-        source, made, out = ((weights, wslots, wgt_out), (products, nslots, num_out))[kind]
-        ring = x if kind == 0 else y
-        there, here = patch_at(ring, core, STEPS[r]), ring * 2 + core
-
-        def sort(j, carry):
-            made[j] = source[table[j]]
-            return carry
-
-        lax.fori_loop(there * CAP, there * CAP + CAP, sort, 0)
-        pairs = ((meta.at[there], facts_out.at[kind, here]), (made.at[pl.ds(there * CAP, CAP)], out.at[here]))
-        for i, (src, dst) in enumerate(pairs):
-            if r == NP - 1:
-                copy = pltpu.make_async_copy(src, dst, own_sem.at[kind, i])
-                copy.start()
-            else:
-                device = along_x(STEPS[r]) if kind == 0 else along_y(STEPS[r])
-                copy = send(src, dst, send_sem.at[kind, i, r], recv_sem.at[kind, i, r], device)
-            copies.append(copy)
-
-    wait(2 * (NP - 1))
-    for r in range(NP):
-        to_patch(0, r)
-
     span = taps.shape[2]
     tap = lax.broadcasted_iota(jnp.int32, (span, 2 * TS), 0) - span // 2
     spot = lax.broadcasted_iota(jnp.int32, (span, 2 * TS), 1)
@@ -182,6 +147,40 @@
             used = (level == column) & (level < counts[v])
             diagonal = jnp.where(used, coefs[c, v : v + 1, :].astype(F32), 0.0).astype(BF16)
             rows[v, c] = jnp.dot(diagonal, jnp.ones((NB, TS), BF16), preferred_element_type=F32)
+    loads[0].wait()
+    loads[1].wait()
+
+    def weigh(i, carry):
+        t = table[NP * CAP + i]
+        weights[i] = jnp.where(bad[t] == 0, 1.0 / var[t].astype(F32), 0.0).astype(BF16)
+        return carry
+
+    copies = []
+
+    def to_patch(kind, r, begin=0, end=CAP):
+        source, made, out = ((weights, wslots, wgt_out), (products, nslots, num_out))[kind]
+        ring = x if kind == 0 else y
+        there, here = patch_at(ring, core, STEPS[r]), ring * 2 + core
+
+        def sort(j, carry):
+            made[j] = source[table[j]]
+            return carry
+
+        lax.fori_loop(there * CAP + begin, there * CAP + end, sort, 0)
+        tiles = made.at[pl.ds(there * CAP + begin, end - begin)], out.at[here, pl.ds(begin, end - begin)]
+        pairs = [(0 if end == CAP else 1, *tiles)]
+        if end == CAP:
+            pairs.append((2, meta.at[there], facts_out.at[kind, here]))
+        for i, src, dst in pairs:
+            if r == NP - 1:
+                copy = pltpu.make_async_copy(src, dst, own_sem.at[kind, i])
+                copy.start()
+            else:
+                device = along_x(STEPS[r]) if kind == 0 else along_y(STEPS[r])
+                copy = send(src, dst, send_sem.at[kind, i, r], recv_sem.at[kind, i, r], device)
+            copies.append(copy)
+
+    lax.fori_loop(0, CAP // 2, weigh, 0)
     loads[2].wait()
 
     row_iota = lax.broadcasted_iota(jnp.int32, (TS, TS), 0)
@@ -219,7 +218,17 @@
             products[2 * step + i] = (weight * matched[i].astype(BF16).astype(F32)).astype(BF16)
         return carry
 
-    for r in range(NT // CAP):
+    lax.fori_loop(0, CAP // 4, pair, 0)
+    wait(2 * (NP - 1))
+    to_patch(1, 0, 0, CAP // 2)
+    lax.fori_loop(CAP // 2, NT, weigh, 0)
+    for r in range(2):
+        to_patch(0, r)
+    lax.fori_loop(CAP // 4, CAP // 2, pair, 0)
+    to_patch(1, 0, CAP // 2)
+    for r in range(2, NP):
+        to_patch(0, r)
+    for r in range(1, NT // CAP):
         lax.fori_loop(r * CAP // 2, (r + 1) * CAP // 2, pair, 0)
         if r < NT // CAP - 1:
             to_patch(1, r)
@@ -250,7 +259,7 @@
             pltpu.VMEM((NB // 2, 2 * TS, 2 * TS), BF16),
             pltpu.VMEM((2 * TS, NB * TS), BF16),
             pltpu.VMEM((2, 3, NB, TS), F32),
-            dma((3,)), dma((2, 2)), dma((2, 2, NP)), dma((2, 2, NP)),
+            dma((3,)), dma((2, 3)), dma((2, 3, NP)), dma((2, 3, NP)),
         ],
         compiler_params=pltpu.CompilerParams(
             collective_id=0, has_side_effects=True, vmem_limit_bytes=54 * 2**20
@@ -259,72 +268,83 @@
     )(*operands)
 
 
-def add_kernel(facts, wgt, num, wgt_sum, num_sum, wgt_window, num_window):
-    source = pl.program_id(0)
-    planes = ((0, wgt, wgt_sum, wgt_window), (1, num, num_sum, num_window))
-
-    @pl.when(source == 0)
-    def _():
-        def clear(i, carry):
-            for plane in planes:
-                plane[3][i] = jnp.zeros((WIN, TS), F32)
-            return carry
-
-        lax.fori_loop(0, WIN // TS + 1, clear, 0)
-
+def add_kernel(facts, wgt, num, wgt_sum, num_sum, wgt_window, num_window, wgt_tiles, num_tiles, sem):
+    planes = ((0, wgt_tiles, wgt_sum, wgt_window), (1, num_tiles, num_sum, num_window))
+
+    def loads(source):
+        part = pl.ds(pl.multiple_of(source * CAP, CAP), CAP)
+        return (
+            pltpu.make_async_copy(wgt.at[part], wgt_tiles.at[part], sem.at[0, source]),
+            pltpu.make_async_copy(num.at[part], num_tiles.at[part], sem.at[1, source]),
+        )
+
+    for source in range(NP):
+        for load in loads(source):
+            load.start()
+
+    def clear(i, carry):
+        for plane in planes:
+            plane[3][i] = jnp.zeros((WIN, TS), F32)
+        return carry
+
+    lax.fori_loop(0, WIN // TS + 1, clear, 0)
     lane = lax.broadcasted_iota(jnp.int32, (TS, TS), 1)
-    for kind, tiles, _, window in planes:
-        work = []
-        for s in range(CAP):
-            j = source * CAP + s
-            used = facts[kind, j, 2]
-            top = pl.multiple_of(facts[kind, j, 0], 8)
-            left = facts[kind, j, 1]
-            shift = lax.rem(left, TS)
-            tile = pltpu.roll(tiles[s].astype(F32), shift, 1)
-            here = lane >= jnp.where(used > 0, shift, TS)
-            there = lane < jnp.where(used > 0, shift, 0)
-            work.append((left // TS, top, tile, here, there))
-        for q, top, tile, here, there in work:
-            window[q, pl.ds(top, TS), :] += jnp.where(here, tile, 0.0)
-            window[q + 1, pl.ds(top, TS), :] += jnp.where(there, tile, 0.0)
-
-    @pl.when(source == NP - 1)
-    def _():
-        _, _, z, _ = place()
-
-        def write(a, carry):
-            for i, k in enumerate(BLOCKS):
-                v = a * NZ + lax.rem(z + k, NZ)
-                for half in range(2):
-                    at = pl.multiple_of((2 * v + half) * SIDE, SIDE)
-                    for _, _, out, window in planes:
-                        for q in range(WIN // TS):
-                            out[a, i, half, :, q * TS : (q + 1) * TS] = window[q, pl.ds(at, SIDE), :].astype(BF16)
-            return carry
-
-        lax.fori_loop(0, NA, write, 0)
+
+    def add(source, carry):
+        arriving = loads(source)
+        for kind, tiles, _, window in planes:
+            arriving[kind].wait()
+            work = []
+            for s in range(CAP):
+                j = source * CAP + s
+                used = facts[kind, j, 2]
+                top = pl.multiple_of(facts[kind, j, 0], 8)
+                left = facts[kind, j, 1]
+                shift = lax.rem(left, TS)
+                tile = pltpu.roll(tiles[j].astype(F32), shift, 1)
+                here = lane >= jnp.where(used > 0, shift, TS)
+                there = lane < jnp.where(used > 0, shift, 0)
+                work.append((left // TS, top, tile, here, there))
+            for q, top, tile, here, there in work:
+                window[q, pl.ds(top, TS), :] += jnp.where(here, tile, 0.0)
+                window[q + 1, pl.ds(top, TS), :] += jnp.where(there, tile, 0.0)
+        return carry
+
+    lax.fori_loop(0, NP, add, 0)
+    _, _, z, _ = place()
+
+    def write(a, carry):
+        for i, k in enumerate(BLOCKS):
+            v = a * NZ + lax.rem(z + k, NZ)
+            for half in range(2):
+                at = pl.multiple_of((2 * v + half) * SIDE, SIDE)
+                for _, _, out, window in planes:
+                    for q in range(WIN // TS):
+                        out[a, i, half, :, q * TS : (q + 1) * TS] = window[q, pl.ds(at, SIDE), :].astype(BF16)
+        return carry
+
+    lax.fori_loop(0, NA, write, 0)
 
 
 def add_tiles(wgt, num, facts):
-    block = pl.BlockSpec((CAP, TS, TS), lambda i: (i, 0, 0))
     out = jax.ShapeDtypeStruct((NA, NZ, 2, SIDE, WIN), BF16)
     tiles = [t.reshape(NP * CAP, TS, TS) for t in (wgt, num)]
     return pl.pallas_call(
         add_kernel,
-        grid=(NP,),
         out_shape=(out, out),
-        in_specs=[SMEM, block, block],
+        in_specs=[SMEM, ANY, ANY],
         out_specs=(VMEM, VMEM),
-        scratch_shapes=[pltpu.VMEM((WIN // TS + 1, WIN, TS), F32)] * 2,
-        compiler_params=pltpu.CompilerParams(vmem_limit_bytes=40 * 2**20),
+        scratch_shapes=[pltpu.VMEM((WIN // TS + 1, WIN, TS), F32)] * 2
+        + [pltpu.VMEM((NP * CAP, TS, TS), BF16)] * 2
+        + [pltpu.SemaphoreType.DMA((2, NP))],
+        compiler_params=pltpu.CompilerParams(vmem_limit_bytes=48 * 2**20),
         name="add_tiles",
     )(facts.reshape(2, NP * CAP, TS), *tiles)
 
 
 class Plane:
-    def __init__(self, a, z, along_a, along_z, src, a_recv, a_send, mid, z_recv, z_send, as_sem, ar_sem, zs_sem, zr_sem):
-        self.a, self.z, self.along_a, self.along_z, self.src = a, z, along_a, along_z, src
+    def __init__(self, a, z, along_a, along_z, owner_z, src, a_recv, a_send, mid, z_recv, z_send, as_sem, ar_sem, zs_sem, zr_sem):
+        self.a, self.z, self.along_a, self.along_z, self.owner_z, self.src = a, z, along_a, along_z, owner_z, src
         self.a_recv, self.a_send, self.mid, self.z_recv, self.z_send = a_recv, a_send, mid, z_recv, z_send
         self.as_sem, self.ar_sem, self.zs_sem, self.zr_sem = as_sem, ar_sem, zs_sem, zr_sem
         self.copies = {}
@@ -373,7 +393,7 @@
     def along(self, j):
         for way in range(2):
             at = BLOCKS.index(4 - j if way == 0 else 4 + j)
-            to = self.along_z(lax.rem(self.z + (1 if way == 0 else NZ - 1), NZ))
+            to = (self.along_z if j < 3 else self.owner_z)(lax.rem(self.z + (1 if way == 0 else NZ - 1), NZ))
             if j == 0:
                 src, dst = self.mid.at[at, way], self.z_recv.at[way, 0, way]
             else:
@@ -387,8 +407,7 @@
                     src[1 - way] = (block[1 - way].astype(F32) + got[1 - way].astype(F32)).astype(BF16)
             self.copies["z", way, j] = send(src, dst, self.zs_sem.at[way, j], self.zr_sem.at[way, j], to)
 
-    def total(self):
-        out = self.ring_sum(NZ - 1)
+    def total(self, out):
         for way in range(2):
             self.copies["z", way, 3].wait_recv()
             out = [value + self.z_recv[way, 3, half].astype(F32) for half, value in enumerate(out)]
@@ -420,27 +439,28 @@
     along_x = lambda to: {"visit": to * NZ + z}
     along_y = lambda to: {"patch": to * 2 + core}
     along_z = lambda to: {"visit": x * NZ + to}
-    swapped = {"patch": x * 2 + core, "visit": y * NZ + z}
-    moved, swap_send, swap_recv = scratch[2 * PLANE_SCRATCH :]
+    swapped = lambda to: {"patch": x * 2 + core, "visit": y * NZ + to}
+    kept, swap_send, swap_recv = scratch[2 * PLANE_SCRATCH :]
 
     for to in (1, NA - 1):
         signal(along_x(lax.rem(x + to, NA)))
         signal(along_y(lax.rem(y + to, NA)))
     for to in (1, NZ - 1):
         signal(along_z(lax.rem(z + to, NZ)))
+        signal(swapped(lax.rem(z + to, NZ)))
 
     @pl.when(x != y)
     def _():
-        signal(swapped)
-        wait(7)
+        signal(swapped(z))
+        wait(9)
 
     @pl.when(x == y)
     def _():
-        wait(6)
+        wait(8)
 
     planes = (
-        Plane(y, z, along_y, along_z, wgt, *scratch[:PLANE_SCRATCH]),
-        Plane(x, z, along_x, along_z, num, *scratch[PLANE_SCRATCH : 2 * PLANE_SCRATCH]),
+        Plane(y, z, along_y, along_z, swapped, wgt, *scratch[:PLANE_SCRATCH]),
+        Plane(x, z, along_x, along_z, along_z, num, *scratch[PLANE_SCRATCH : 2 * PLANE_SCRATCH]),
     )
     for i in range(len(FAR_PIECES)):
         for plane in planes:
@@ -456,18 +476,29 @@
         if i < NZ // 2:
             for plane in planes:
                 plane.along(i)
-    total = planes[0].total()
+    planes[0].keep(NZ - 1)
+    own = planes[0].mid.at[NZ - 1]
+    swap = pltpu.make_async_remote_copy(
+        src_ref=own, dst_ref=kept, send_sem=swap_send, recv_sem=swap_recv, device_id=swapped(z), device_id_type=MESH
+    )
 
     @pl.when(x != y)
     def _():
-        moved[...] = total
-        send(moved, depth, swap_send, swap_recv, swapped).wait()
+        swap.start()
 
     @pl.when(x == y)
     def _():
-        depth[...] = total
-
-    coadd[...] = planes[1].total() / jnp.maximum(depth[...], 1.0)
+        kept[...] = own[...]
+
+    mine = planes[1].total(planes[1].ring_sum(NZ - 1))
+
+    @pl.when(x != y)
+    def _():
+        swap.wait()
+
+    total = planes[0].total([kept[half].astype(F32) for half in range(2)])
+    depth[...] = total
+    coadd[...] = mine / jnp.maximum(total, 1.0)
     for plane in planes:
         plane.finish()
 
@@ -481,7 +512,7 @@
         out_specs=(VMEM, VMEM),
         scratch_shapes=plane_scratch()
         + plane_scratch()
-        + [pltpu.VMEM((2 * SIDE, WIN), F32), pltpu.SemaphoreType.DMA, pltpu.SemaphoreType.DMA],
+        + [pltpu.VMEM((2, SIDE, WIN), BF16), pltpu.SemaphoreType.DMA, pltpu.SemaphoreType.DMA],
         compiler_params=pltpu.CompilerParams(
             collective_id=1, has_side_effects=True, vmem_limit_bytes=40 * 2**20
         ),

time: 88.9 us -> 83.8 us (0.943)
  local copies, waits for them, and re-layouts: 5.33 us -> 2.15 us
  Pallas kernels: 81.9 us -> 80.3 us
    unnamed x8 -> x4, local copies, waits for them, and re-layouts: 5.33 us -> 2.15 us
    pallas_call x1, Pallas kernels: 34.4 us -> 33 us  [match(): pl.pallas_call(match_kernel, out_shape=(got, got, facts), in_specs=[SMEM,...]
    pallas_call x1, Pallas kernels: 40.1 us -> 39.2 us  [sum_windows(): pl.pallas_call(sum_kernel, out_shape=(out, out), in_specs=[VMEM, VMEM], o...]
where the time goes in v3:
time: 83.8 us; the launch traced here: 83.2 us
  Pallas kernels  80.3 us (96%)
  local copies, waits for them, and re-layouts  2.15 us (3%)
    pallas_call x1, Pallas kernels, sum_windows(): pl.pallas_call(sum_kernel, out_shape=(out, out), in_specs=[VMEM, VMEM], o...  39.2 us
    pallas_call x1, Pallas kernels, match(): pl.pallas_call(match_kernel, out_shape=(got, got, facts), in_specs=[SMEM,...  33 us
    pallas_call x1, Pallas kernels, add_tiles(): pl.pallas_call(add_kernel, out_shape=(out, out), in_specs=[SMEM, ANY, ANY...  6.07 us
    unnamed x4, local copies, waits for them, and re-layouts  2.15 us
    pallas_call x1, Pallas kernels, slots(): pl.pallas_call(slot_kernel, out_shape=(jax.ShapeDtypeStruct((NP * CAP + N...  2.09 us

profile of v3, /device:TPU:24, one launch (start us, length us, event | category | flops | bytes accessed | tf_op | source)
XLA Modules:
  0.0 83.2 jit_solution(5182455737632587116)
XLA Ops:
  0.6 2.1 %slots.1 = (s32[96]{0:T(128)}, s32[8,8,128]{2,1,0:T(8,128)}) custom-call(s32[1,32]{1,0:T(1,128)} %bitcast.12, s32[2,32]{1,0:T(2,128)} %bitcast.10), custom_call_target="tpu_custom_call" | custom-call | tf_op jit(solution)/shard_map/slots/pallas_call | solution.py:92
  2.7 33.0 %match_tiles.1 = (bf16[8,8,128,128]{3,2,1,0:T(8,128)(2,1)}, bf16[8,8,128,128]{3,2,1,0:T(8,128)(2,1)}, s32[2,8,8,128]{3,2,1,0:T(8,128)}) custom-call(s32[96]{0:T(128)} %get-tuple-element.9.table, s32[2,32]{1,0:T(2,128)} %bitcast.11, s32[32]{0:T(128)} %visits.1, s32[2]{0:T(128)} %counts.1, bf16[3,2,16]{2,1,0:T(2,128)(2,1)} %bitcast.9, ...), custom_call_target="tpu_custom_call" | custom-call | tf_op jit(solution)/shard_map/match_tiles/pallas_call | solution.py:245
  35.8 0.0 copy-start
  35.8 0.8 copy-done
  36.6 6.1 %add_tiles.1 = (bf16[4,8,2,16,1024]{4,3,2,1,0:T(8,128)(2,1)S(1)}, bf16[4,8,2,16,1024]{4,3,2,1,0:T(8,128)(2,1)S(1)}) custom-call(s32[2,64,128]{2,1,0:T(8,128)S(1)} %bitcast.6, bf16[64,128,128]{2,1,0:T(8,128)(2,1)} %bitcast.7, bf16[64,128,128]{2,1,0:T(8,128)(2,1)} %bitcast.8), custom_call_target="tpu_custom_call" | custom-call | tf_op jit(solution)/shard_map/add_tiles/pallas_call | solution.py:332
  42.7 39.2 %sum_windows.1 = (f32[32,1024]{1,0:T(8,128)S(1)}, f32[32,1024]{1,0:T(8,128)S(1)}) custom-call(bf16[4,8,2,16,1024]{4,3,2,1,0:T(8,128)(2,1)S(1)} %get-tuple-element.14.wgt, bf16[4,8,2,16,1024]{4,3,2,1,0:T(8,128)(2,1)S(1)} %get-tuple-element.15.num), custom_call_target="tpu_custom_call" | custom-call | tf_op jit(solution)/shard_map/sum_windows/pallas_call | solution.py:508
  81.8 0.7 copy.13
  82.5 0.7 copy.14
Async XLA Ops:
  35.8 0.8 %copy-start = (s32[2,8,8,128]{3,2,1,0:T(8,128)S(1)}, s32[2,8,8,128]{3,2,1,0:T(8,128)}, u32[]{:S(2)}) copy-start(s32[2,8,8,128]{3,2,1,0:T(8,128)} %get-tuple-element.11) | copy-start | bytes 196612

commit v4 on v3

--- a/solution.py
+++ b/solution.py
@@ -268,7 +268,9 @@
     )(*operands)
 
 
-def add_kernel(facts, wgt, num, wgt_sum, num_sum, wgt_window, num_window, wgt_tiles, num_tiles, sem):
+def add_kernel(
+    facts_in, wgt, num, wgt_sum, num_sum, wgt_window, num_window, wgt_tiles, num_tiles, facts, facts_sem, sem
+):
     planes = ((0, wgt_tiles, wgt_sum, wgt_window), (1, num_tiles, num_sum, num_window))
 
     def loads(source):
@@ -278,6 +280,8 @@
             pltpu.make_async_copy(num.at[part], num_tiles.at[part], sem.at[1, source]),
         )
 
+    facts_load = pltpu.make_async_copy(facts_in, facts, facts_sem)
+    facts_load.start()
     for source in range(NP):
         for load in loads(source):
             load.start()
@@ -288,6 +292,7 @@
         return carry
 
     lax.fori_loop(0, WIN // TS + 1, clear, 0)
+    facts_load.wait()
     lane = lax.broadcasted_iota(jnp.int32, (TS, TS), 1)
 
     def add(source, carry):
@@ -332,11 +337,15 @@
     return pl.pallas_call(
         add_kernel,
         out_shape=(out, out),
-        in_specs=[SMEM, ANY, ANY],
+        in_specs=[ANY, ANY, ANY],
         out_specs=(VMEM, VMEM),
         scratch_shapes=[pltpu.VMEM((WIN // TS + 1, WIN, TS), F32)] * 2
         + [pltpu.VMEM((NP * CAP, TS, TS), BF16)] * 2
-        + [pltpu.SemaphoreType.DMA((2, NP))],
+        + [
+            pltpu.SMEM((2, NP * CAP, TS), jnp.int32),
+            pltpu.SemaphoreType.DMA,
+            pltpu.SemaphoreType.DMA((2, NP)),
+        ],
         compiler_params=pltpu.CompilerParams(vmem_limit_bytes=48 * 2**20),
         name="add_tiles",
     )(facts.reshape(2, NP * CAP, TS), *tiles)

time: 83.8 us -> 82.9 us (0.989)
  Pallas kernels: 80.3 us -> 79.4 us
    pallas_call x1, Pallas kernels: 6.07 us -> 5.14 us  [add_tiles(): pl.pallas_call(add_kernel, out_shape=(out, out), in_specs=[ANY, ANY, ANY]...]
where the time goes in v4:
time: 82.9 us; the launch traced here: 82.2 us
  Pallas kernels  79.4 us (96%)
  local copies, waits for them, and re-layouts  2.15 us (3%)
    pallas_call x1, Pallas kernels, sum_windows(): pl.pallas_call(sum_kernel, out_shape=(out, out), in_specs=[VMEM, VMEM], o...  39.2 us
    pallas_call x1, Pallas kernels, match(): pl.pallas_call(match_kernel, out_shape=(got, got, facts), in_specs=[SMEM,...  33 us
    pallas_call x1, Pallas kernels, add_tiles(): pl.pallas_call(add_kernel, out_shape=(out, out), in_specs=[ANY, ANY, ANY]...  5.14 us
    unnamed x4, local copies, waits for them, and re-layouts  2.15 us
    pallas_call x1, Pallas kernels, slots(): pl.pallas_call(slot_kernel, out_shape=(jax.ShapeDtypeStruct((NP * CAP + N...  2.09 us

profile of v4, /device:TPU:24, one launch (start us, length us, event | category | flops | bytes accessed | tf_op | source)
XLA Modules:
  0.0 82.2 jit_solution(11471449964067420716)
XLA Ops:
  0.6 2.1 %slots.1 = (s32[96]{0:T(128)}, s32[8,8,128]{2,1,0:T(8,128)}) custom-call(s32[1,32]{1,0:T(1,128)} %bitcast.12, s32[2,32]{1,0:T(2,128)} %bitcast.10), custom_call_target="tpu_custom_call" | custom-call | tf_op jit(solution)/shard_map/slots/pallas_call | solution.py:92
  2.7 33.0 %match_tiles.1 = (bf16[8,8,128,128]{3,2,1,0:T(8,128)(2,1)}, bf16[8,8,128,128]{3,2,1,0:T(8,128)(2,1)}, s32[2,8,8,128]{3,2,1,0:T(8,128)}) custom-call(s32[96]{0:T(128)} %get-tuple-element.9.table, s32[2,32]{1,0:T(2,128)} %bitcast.11, s32[32]{0:T(128)} %visits.1, s32[2]{0:T(128)} %counts.1, bf16[3,2,16]{2,1,0:T(2,128)(2,1)} %bitcast.9, ...), custom_call_target="tpu_custom_call" | custom-call | tf_op jit(solution)/shard_map/match_tiles/pallas_call | solution.py:245
  35.8 0.0 copy-start
  35.8 0.8 %copy-done = s32[2,8,8,128]{3,2,1,0:T(8,128)S(1)} copy-done((s32[2,8,8,128]{3,2,1,0:T(8,128)S(1)}, s32[2,8,8,128]{3,2,1,0:T(8,128)}, u32[]{:S(2)}) %copy-start) | copy-done | bytes 65560
  36.6 5.1 %add_tiles.1 = (bf16[4,8,2,16,1024]{4,3,2,1,0:T(8,128)(2,1)S(1)}, bf16[4,8,2,16,1024]{4,3,2,1,0:T(8,128)(2,1)S(1)}) custom-call(s32[2,64,128]{2,1,0:T(8,128)S(1)} %bitcast.6, bf16[64,128,128]{2,1,0:T(8,128)(2,1)} %bitcast.7, bf16[64,128,128]{2,1,0:T(8,128)(2,1)} %bitcast.8), custom_call_target="tpu_custom_call" | custom-call | tf_op jit(solution)/shard_map/add_tiles/pallas_call | solution.py:337
  41.8 39.2 %sum_windows.1 = (f32[32,1024]{1,0:T(8,128)S(1)}, f32[32,1024]{1,0:T(8,128)S(1)}) custom-call(bf16[4,8,2,16,1024]{4,3,2,1,0:T(8,128)(2,1)S(1)} %get-tuple-element.14.wgt, bf16[4,8,2,16,1024]{4,3,2,1,0:T(8,128)(2,1)S(1)} %get-tuple-element.15.num), custom_call_target="tpu_custom_call" | custom-call | tf_op jit(solution)/shard_map/sum_windows/pallas_call | solution.py:517
  80.9 0.7 copy.13
  81.6 0.7 copy.14
Async XLA Ops:
  35.8 0.8 %copy-start = (s32[2,8,8,128]{3,2,1,0:T(8,128)S(1)}, s32[2,8,8,128]{3,2,1,0:T(8,128)}, u32[]{:S(2)}) copy-start(s32[2,8,8,128]{3,2,1,0:T(8,128)} %get-tuple-element.11) | copy-start | bytes 196612
